TPU v7x, 32 devices: a whole 2x2x4 slice. The times are simulated.
32 devices in a mesh: member: 4 (over x, core), space: 8 (over z, y).
Axes of the slice: x: 2, y: 2, z: 4, core: 2. Of those that a mesh axis runs over, the one named last changes fastest.
Arguments:
- members: bfloat16 [64, 32, 128, 384], P('member', None, 'space'), may hold values from -6 to 6
- control: float32 [32, 128, 384], P(None, 'space'), may hold values from -6 to 6
- hybrid_weight: float32 [32], replicated, may hold values from 0.2 to 0.6
- member_weights: int32 [64], replicated, may hold values from 1 to 8
- source_device: int32 [128, 1], P('space'), may hold values from 0 to 7, as said below
- source_row: int32 [128], P('space'), may hold values from 0 to 15
- column_source: int32 [128, 768], P('space'), may hold values from 0 to 382, as said below
- column_code: int32 [128, 768], P('space'), may hold values from 0 to 16
Outputs:
- fine_increment: float32 [128, 32, 2, 768], P('space', 'member')
Inputs may be any that keep to these rules, and one draw needn't show every extreme that they name: `source_device`: among the 16 fine blocks of one device no space index is named more than 4 times, and in every draw some device's blocks name some index exactly 4 times. `column_source`: within 2 of (j - 1) // 2 for fine column j, clipped to the range.
All inputs are finite; a program needn't handle non-finite values.
Results may differ from a plain program's by a relative error of at most 0.0022.
Values sent between devices are 32-bit elements; how exact they have to be, the bound alone decides.
A program may use at most 128 MiB of HBM per device.

v0:
```python
import functools

import jax
import jax.numpy as jnp
from jax import lax
from jax.experimental import pallas as pl
from jax.experimental.pallas import tpu as pltpu
from jax.sharding import PartitionSpec as P

SWEEPS = 4
DIFFUSE = 0.2
SCALE = DIFFUSE**SWEEPS
REACH = SWEEPS // 2
LANES = 128
MESH = pl.DeviceIdType.MESH


def beside(x):
    width = x.shape[-1]
    lane = lax.broadcasted_iota(jnp.int32, x.shape, x.ndim - 1)
    left = jnp.where(lane == 0, 0.0, pltpu.roll(x, 1, x.ndim - 1))
    right = jnp.where(lane == width - 1, 0.0, pltpu.roll(x, width - 1, x.ndim - 1))
    return left + right


def apply_kernel(
    spaces,
    slots,
    members,
    control,
    edges,
    own,
    weight,
    blend,
    request,
    arrived,
    perm,
    states,
    stage_up,
    stage_down,
    recv_low,
    recv_high,
    ctrl_low,
    ctrl_high,
    ext_x,
    buf_a,
    buf_b,
    stat_a,
    stat_b,
    acc,
    red,
    ext,
    from_low,
    from_high,
    fin,
    asked,
    outgoing,
    load_sem,
    up_send,
    up_recv,
    down_send,
    down_recv,
    edge_send,
    edge_recv,
    ask_send,
    ask_recv,
    red_send,
    red_recv,
    fix_send,
    fix_recv,
    out_send,
    out_recv,
    own_sem,
):
    me = lax.axis_index("space")
    slot = lax.axis_index("member")
    count, chans, rows, width = members.shape
    own_chans = chans // slots
    capacity = request.shape[1]
    has_low = me > 0
    has_high = me < spaces - 1
    low_mask = jnp.where(has_low, 1.0, 0.0).astype(jnp.float32)
    high_mask = jnp.where(has_high, 1.0, 0.0).astype(jnp.float32)
    low, high = {"space": me - 1}, {"space": me + 1}

    def load(group):
        owner = lax.rem(slot + 1 + group, slots)
        first = pl.multiple_of(owner * own_chans, own_chans)
        return pltpu.make_async_copy(
            members.at[:, pl.ds(first, own_chans)], states.at[group], load_sem.at[group]
        )

    for group in range(slots):
        load(group).start()

    barrier = pltpu.get_barrier_semaphore()
    for step in range(1, spaces):
        pl.semaphore_signal(
            barrier, inc=1, device_id={"space": lax.rem(me + step, spaces)}, device_id_type=MESH
        )
    for step in range(1, slots):
        pl.semaphore_signal(
            barrier, inc=1, device_id={"member": lax.rem(slot + step, slots)}, device_id_type=MESH
        )

    place = lax.broadcasted_iota(jnp.int32, perm.shape, 0)
    source = lax.broadcasted_iota(jnp.int32, perm.shape, 1)
    wanted = lax.rem(place, count) * rows + place // count
    perm[...] = jnp.where(source == wanted, 1.0, 0.0).astype(jnp.bfloat16)

    pl.semaphore_wait(barrier, spaces + slots - 2)

    def remote(src, dst, send, recv, device):
        return pltpu.make_async_remote_copy(
            src_ref=src,
            dst_ref=dst,
            send_sem=send,
            recv_sem=recv,
            device_id=device,
            device_id_type=MESH,
        )

    def edge_up():
        return remote(
            edges.at[pl.ds(0, REACH)], ctrl_high, edge_send.at[0], edge_recv.at[0], low
        )

    def edge_down():
        return remote(
            edges.at[pl.ds(REACH, REACH)], ctrl_low, edge_send.at[1], edge_recv.at[1], high
        )

    def halo_up(turn):
        return remote(
            stage_up.at[turn], recv_high.at[turn], up_send.at[turn], up_recv.at[turn], low
        )

    def halo_down(turn):
        return remote(
            stage_down.at[turn], recv_low.at[turn], down_send.at[turn], down_recv.at[turn], high
        )

    def ask(step):
        target = lax.rem(me + step, spaces)
        return remote(
            request.at[target],
            asked.at[step - 1],
            ask_send.at[step - 1],
            ask_recv.at[step - 1],
            {"space": target},
        )

    @pl.when(has_low)
    def _():
        edge_up().start()

    @pl.when(has_high)
    def _():
        edge_down().start()

    span = REACH * count
    for group in range(slots):
        load(group).wait()

        def send_edges(index, carry, group=group):
            turn = group * own_chans + index
            flat = states[group, :, index].reshape(count * rows, width)
            picks = jnp.concatenate(
                [perm[pl.ds(0, span), :], perm[pl.ds((rows - REACH) * count, span), :]], axis=0
            )
            both = jnp.dot(picks, flat, preferred_element_type=jnp.float32)
            stage_up[turn] = both[:span]
            stage_down[turn] = both[span:]

            @pl.when(has_low)
            def _():
                halo_up(turn).start()

            @pl.when(has_high)
            def _():
                halo_down(turn).start()

            return carry

        lax.fori_loop(0, own_chans, send_edges, 0)

    for step in range(1, spaces):
        ask(step).start()

    @pl.when(jnp.logical_not(has_low))
    def _():
        recv_low[...] = jnp.zeros_like(recv_low)
        ctrl_low[...] = jnp.zeros_like(ctrl_low)
        from_low[...] = jnp.zeros_like(from_low)

    @pl.when(jnp.logical_not(has_high))
    def _():
        recv_high[...] = jnp.zeros_like(recv_high)
        ctrl_high[...] = jnp.zeros_like(ctrl_high)
        from_high[...] = jnp.zeros_like(from_high)

    def swept(ref, at):
        middle = ref[at]
        return ref[at - 1] + ref[at + 1] + (middle + beside(middle))

    def masked(value, row):
        if row < 0:
            return value * low_mask
        if row >= rows:
            return value * high_mask
        return value

    stat_a[...] = jnp.zeros_like(stat_a)
    stat_b[...] = jnp.zeros_like(stat_b)
    margin = SWEEPS + 1
    for row in range(rows):
        stat_a[margin + row] = own[row]
    here, there = stat_a, stat_b
    for sweep in range(1, SWEEPS + 1):
        for row in range(-sweep, rows + sweep):
            there[margin + row] = masked(swept(here, margin + row), row)
        here, there = there, here
    static = here

    buf_a[...] = jnp.zeros_like(buf_a)
    buf_b[...] = jnp.zeros_like(buf_b)
    base = REACH + 2

    @pl.when(has_low)
    def _():
        edge_down().wait_recv()

    @pl.when(has_high)
    def _():
        edge_up().wait_recv()

    def give(group):
        return remote(
            acc.at[group],
            red.at[group],
            red_send.at[group],
            red_recv.at[group],
            {"member": lax.rem(slot + 1 + group, slots)},
        )

    for group in range(slots):
        owner = lax.rem(slot + 1 + group, slots)

        def one_channel(index, carry, group=group, owner=owner):
            turn = group * own_chans + index
            chan = owner * own_chans + index
            flat = states[group, :, index].reshape(count * rows, width)
            ext_x[pl.ds(REACH * count, rows * count), :] = jnp.dot(
                perm[...], flat, preferred_element_type=jnp.float32
            )

            @pl.when(has_low)
            def _():
                halo_down(turn).wait_recv()

            @pl.when(has_high)
            def _():
                halo_up(turn).wait_recv()

            ext_x[pl.ds(0, span), :] = recv_low[turn]
            ext_x[pl.ds((rows + REACH) * count, span), :] = recv_high[turn]

            def state(row):
                return ext_x[pl.ds((row + REACH) * count, count), :]

            for row in range(-REACH, rows + REACH):
                if row < 0:
                    line = ctrl_low[row + REACH, pl.ds(chan, 1), :]
                elif row >= rows:
                    line = ctrl_high[row - rows, pl.ds(chan, 1), :]
                else:
                    line = control[chan, pl.ds(row, 1), :]
                buf_a[base + row] = state(row) * line

            def collect(row, value):
                total = jnp.sum(state(row) * value * weight[...], axis=0, keepdims=True)
                acc[group, row + REACH, pl.ds(index, 1), :] = total

            for outer, inner, away in ((-1, 2, 1), (rows, rows - 3, -1)):
                near = buf_a[base + inner]
                far = buf_a[base + inner + away]
                collect(outer, SWEEPS * (near + beside(near)) + far)
                collect(outer - away, near)

            for row in range(-3, rows + 3):
                buf_b[base + row] = masked(swept(buf_a, base + row), row)
            for row in range(-2, rows + 2):
                buf_a[base + row] = masked(swept(buf_b, base + row), row)
            for row in range(-1, rows + 1):
                buf_b[base + row] = masked(swept(buf_a, base + row), row)
            for row in range(rows):
                collect(row, swept(buf_b, base + row))
            return carry

        lax.fori_loop(0, own_chans, one_channel, 0)
        if group < slots - 1:
            give(group).start()

    for group in range(slots - 1):
        give(group).wait_recv()
    share = blend[...]
    for row in range(-SWEEPS, rows + SWEEPS):
        value = (share * SCALE) * static[margin + row]
        if -REACH <= row < rows + REACH:
            total = acc[slots - 1, row + REACH]
            for group in range(slots - 1):
                total = total + red[group, row + REACH]
            value = value + (1.0 - share) * total
        ext[row + SWEEPS] = value

    def fix_up():
        return remote(
            ext.at[pl.ds(0, SWEEPS + 1)], from_high, fix_send.at[0], fix_recv.at[0], low
        )

    def fix_down():
        return remote(
            ext.at[pl.ds(rows + SWEEPS, SWEEPS)], from_low, fix_send.at[1], fix_recv.at[1], high
        )

    @pl.when(has_low)
    def _():
        fix_up().start()

    @pl.when(has_high)
    def _():
        fix_down().start()

    @pl.when(has_low)
    def _():
        fix_down().wait_recv()

    @pl.when(has_high)
    def _():
        fix_up().wait_recv()

    for row in range(rows + 1):
        value = ext[row + SWEEPS]
        if row < SWEEPS:
            value = value + from_low[row]
        if row >= rows - SWEEPS:
            value = value + from_high[row - rows + SWEEPS]
        fin[row] = value

    def answer(step):
        target = lax.rem(me + spaces - step, spaces)
        return remote(
            outgoing.at[step],
            arrived.at[me],
            out_send.at[step - 1],
            out_recv.at[step - 1],
            {"space": target},
        )

    def keep():
        return pltpu.make_async_copy(outgoing.at[0], arrived.at[me], own_sem)

    def fill(step, wants):
        for place in range(capacity):
            line = wants[place]
            line = jnp.concatenate([line] * (width // LANES), axis=1)
            line = jnp.broadcast_to(line, (own_chans, width))
            lower, upper = fin[0], fin[1]
            for row in range(1, rows):
                hit = line == row
                lower = jnp.where(hit, fin[row], lower)
                upper = jnp.where(hit, fin[row + 1], upper)
            outgoing[step, place, 0] = lower
            outgoing[step, place, 1] = upper

    for step in range(1, spaces):
        ask(step).wait_recv()
    for step in range(1, spaces):
        fill(step, [asked[step - 1, pl.ds(place, 1), :] for place in range(capacity)])
        answer(step).start()
    fill(0, [request[me, pl.ds(place, 1), :] for place in range(capacity)])
    keep().start()

    for step in range(1, spaces):
        answer(step).wait_recv()
    keep().wait()
    for step in range(1, spaces):
        answer(step).wait_send()
        ask(step).wait_send()
    for group in range(slots - 1):
        give(group).wait_send()

    @pl.when(has_low)
    def _():
        edge_up().wait_send()
        fix_up().wait_send()

    @pl.when(has_high)
    def _():
        edge_down().wait_send()
        fix_down().wait_send()

    def drain(turn, carry):
        @pl.when(has_low)
        def _():
            halo_up(turn).wait_send()

        @pl.when(has_high)
        def _():
            halo_down(turn).wait_send()

        return carry

    lax.fori_loop(0, chans, drain, 0)


def regrid_kernel(slot_index, column_source, column_code, arrived, out):
    blocks, _, fine = column_source.shape
    chans, width = arrived.shape[2], arrived.shape[3]
    tiles = width // LANES

    def one_block(block, carry):
        at = slot_index[block]
        lower = arrived[at, 0]
        upper = arrived[at, 1]
        pair = (0.75 * lower + 0.25 * upper, 0.25 * lower + 0.75 * upper)
        for tile in range(fine // LANES):
            columns = pl.ds(tile * LANES, LANES)
            left = jnp.broadcast_to(column_source[block, :, columns], (chans, LANES))
            code = jnp.broadcast_to(column_code[block, :, columns], (chans, LANES))
            right_weight = code.astype(jnp.float32) / 16.0
            first = max(0, (tile * LANES - 1) // 2 - 2) // LANES
            last = min(width - 1, ((tile + 1) * LANES - 2) // 2 + 3) // LANES

            def value(field, index):
                found = None
                for part in range(first, min(last, tiles - 1) + 1):
                    piece = field[:, part * LANES : (part + 1) * LANES]
                    got = jnp.take_along_axis(piece, lax.rem(index, LANES), axis=1)
                    if found is None:
                        found = got
                    else:
                        found = jnp.where(index >= part * LANES, got, found)
                return found

            for half in range(2):
                out[block, :, half, columns] = (1.0 - right_weight) * value(
                    pair[half], left
                ) + right_weight * value(pair[half], left + 1)
        return carry

    lax.fori_loop(0, blocks, one_block, 0)


def per_device(
    members,
    control,
    hybrid_weight,
    member_weights,
    source_device,
    source_row,
    column_source,
    column_code,
):
    count, chans, rows, width = members.shape
    spaces, slots = lax.axis_size("space"), lax.axis_size("member")
    slot = lax.axis_index("member")
    own_chans = chans // slots
    capacity = max(2, 2 * rows // spaces)
    f32 = jnp.float32

    codes = member_weights.astype(f32)
    share = lax.dynamic_slice_in_dim(codes, slot * count, count) / jnp.sum(codes)
    weight = jnp.broadcast_to((share * SCALE)[:, None], (count, width))
    blend = lax.dynamic_slice_in_dim(hybrid_weight, slot * own_chans, own_chans)
    blend = jnp.broadcast_to(blend[:, None], (own_chans, width))
    edges = jnp.concatenate([control[:, :REACH], control[:, rows - REACH :]], axis=1)
    edges = jnp.swapaxes(edges, 0, 1)
    own = lax.dynamic_slice_in_dim(control, slot * own_chans, own_chans, 0)
    own = jnp.swapaxes(own, 0, 1)

    source = source_device[:, 0]
    order = jnp.arange(rows, dtype=jnp.int32)
    same = (source[:, None] == source[None, :]) & (order[None, :] < order[:, None])
    slot_index = source * capacity + jnp.sum(same.astype(jnp.int32), axis=1)
    matches = slot_index[None, :] == jnp.arange(spaces * capacity, dtype=jnp.int32)[:, None]
    request = jnp.sum(jnp.where(matches, source_row[None, :], 0), axis=1)
    request = jnp.broadcast_to(
        request.reshape(spaces, capacity)[:, :, None], (spaces, capacity, LANES)
    )

    vmem = pl.BlockSpec(memory_space=pltpu.VMEM)
    anywhere = pl.BlockSpec(memory_space=pl.ANY)
    dma = pltpu.SemaphoreType.DMA
    halo = pltpu.VMEM((chans, REACH * count, width), f32)
    line = pltpu.VMEM((REACH, chans, width), f32)
    ext_rows = rows + 2 * REACH
    arrived = pl.pallas_call(
        functools.partial(apply_kernel, spaces, slots),
        out_shape=jax.ShapeDtypeStruct((spaces, capacity, 2, own_chans, width), f32),
        in_specs=[anywhere] + [vmem] * 6,
        out_specs=anywhere,
        scratch_shapes=[
            pltpu.VMEM((rows * count, rows * count), jnp.bfloat16),
            pltpu.VMEM((slots, count, own_chans, rows, width), jnp.bfloat16),
            halo,
            halo,
            halo,
            halo,
            line,
            line,
            pltpu.VMEM((ext_rows * count, width), f32),
            pltpu.VMEM((rows + 2 * (REACH + 2), count, width), f32),
            pltpu.VMEM((rows + 2 * (REACH + 2), count, width), f32),
            pltpu.VMEM((rows + 2 * (SWEEPS + 1), own_chans, width), f32),
            pltpu.VMEM((rows + 2 * (SWEEPS + 1), own_chans, width), f32),
            pltpu.VMEM((slots, ext_rows, own_chans, width), f32),
            pltpu.VMEM((slots - 1, ext_rows, own_chans, width), f32),
            pltpu.VMEM((rows + 2 * SWEEPS, own_chans, width), f32),
            pltpu.VMEM((SWEEPS, own_chans, width), f32),
            pltpu.VMEM((SWEEPS + 1, own_chans, width), f32),
            pltpu.VMEM((rows + 1, own_chans, width), f32),
            pltpu.VMEM((spaces - 1, capacity, LANES), jnp.int32),
            pltpu.VMEM((spaces, capacity, 2, own_chans, width), f32),
            dma((slots,)),
            dma((chans,)),
            dma((chans,)),
            dma((chans,)),
            dma((chans,)),
            dma((2,)),
            dma((2,)),
            dma((spaces - 1,)),
            dma((spaces - 1,)),
            dma((slots - 1,)),
            dma((slots - 1,)),
            dma((2,)),
            dma((2,)),
            dma((spaces - 1,)),
            dma((spaces - 1,)),
            dma,
        ],
        compiler_params=pltpu.CompilerParams(
            collective_id=0, has_side_effects=True, vmem_limit_bytes=48 * 2**20
        ),
        name="covariance_apply",
    )(members, control, edges, own, weight, blend, request)

    arrived = arrived.reshape(spaces * capacity, 2, own_chans, width)
    return pl.pallas_call(
        regrid_kernel,
        out_shape=jax.ShapeDtypeStruct((rows, own_chans, 2, column_source.shape[1]), f32),
        in_specs=[pl.BlockSpec(memory_space=pltpu.SMEM)] + [vmem] * 3,
        out_specs=vmem,
        compiler_params=pltpu.CompilerParams(vmem_limit_bytes=32 * 2**20),
        name="regrid",
    )(slot_index, column_source[:, None], column_code[:, None], arrived)


def solution(mesh):
    placed = (
        P("member", None, "space", None),
        P(None, "space", None),
        P(),
        P(),
        P("space", None),
        P("space"),
        P("space", None),
        P("space", None),
    )
    return jax.shard_map(
        per_device,
        mesh=mesh,
        in_specs=placed,
        out_specs=P("space", "member", None, None),
        check_vma=False,
    )
```

profile of v0, /device:TPU:0, one launch (start us, length us, event | category | flops | bytes accessed | tf_op | source)
XLA Modules:
  0.0 127.6 jit_solution(3171621545341158673)
XLA Ops:
  0.0 1.3 convert_reduce_fusion.1
  1.3 0.7 dynamic_slice.11
  2.0 0.9 convert_reduce_fusion
  2.9 0.7 multiply_add_fusion.slot_index
  3.6 0.7 select_reduce_fusion
  4.3 0.7 convert_element_type.7
  5.0 0.7 divide_multiply_fusion
  5.7 0.1 broadcast_in_dim.48
  5.8 0.1 broadcast_in_dim.45.blend
  5.8 0.1 broadcast_in_dim.49.request
  5.9 0.1 broadcast_in_dim.44.weight
  6.0 0.8 broadcast_in_dim.24.column_source
  6.8 0.8 broadcast_in_dim.25.column_code
  7.7 0.9 constant_dynamic-slice_fusion
  8.6 0.1 copy.22
  8.7 1.2 fusion.1
  9.9 0.0 copy-start
  9.9 1.1 copy-done
  11.1 112.4 %covariance_apply.1 = f32[8,4,2,8,384]{4,3,2,1,0:T(8,128)S(1)} custom-call(bf16[16,32,16,384]{3,2,1,0:T(8,128)(2,1)} %members.1, f32[32,16,384]{2,1,0:T(8,128)S(1)} %copy-done, f32[4,32,384]{2,1,0:T(8,128)S(1)} %maximum_bitcast_fusion.edges, f32[16,8,384]{2,1,0:T(8,128)S(1)} %bitcast.9, f32[16,384]{1,0:T(8,128)S(1)} %broadcast_in_dim.44.weight, ...), custom_call_target="tpu_custom_call" | custom-call | tf_op jit(solution)/shard_map/covariance_apply/pallas_call | solution.py:498
  123.4 4.2 %regrid.1 = f32[16,8,2,768]{3,2,1,0:T(2,128)} custom-call(s32[16]{0:T(128)S(1)} %multiply_add_fusion.slot_index, s32[16,1,768]{2,1,0:T(1,128)S(1)} %broadcast_in_dim.24.column_source, s32[16,1,768]{2,1,0:T(1,128)S(1)} %broadcast_in_dim.25.column_code, f32[32,2,8,384]{3,2,1,0:T(8,128)S(1)} %bitcast.8), custom_call_target="tpu_custom_call" | custom-call | tf_op jit(solution)/shard_map/regrid/pallas_call | solution.py:549
  (3 shorter events, 0.0 us)
Async XLA Ops:
  9.9 1.1 copy-start
where the time goes:
time: 128 us
  Pallas kernels  117 us (91%)
  local copies, waits for them, and re-layouts  6.04 us (5%)
  other arithmetic  4.97 us (4%)
    pallas_call x1, Pallas kernels, per_device(): pl.pallas_call(functools.partial(apply_kernel, spaces, slots), out_shape=...  112 us
    pallas_call x1, Pallas kernels, per_device(): pl.pallas_call(regrid_kernel, out_shape=jax.ShapeDtypeStruct((rows, own_c...  4.16 us

commit v1 on v0

v1 whole, which is shorter than its diff:
```python
import functools

import jax
import jax.numpy as jnp
from jax import lax
from jax.experimental import pallas as pl
from jax.experimental.pallas import tpu as pltpu
from jax.sharding import PartitionSpec as P

SWEEPS = 4
DIFFUSE = 0.2
SCALE = DIFFUSE**SWEEPS
REACH = SWEEPS // 2
LANES = 128
GROUP = 8
PARTS = 2
AHEAD = 1
MESH = pl.DeviceIdType.MESH


def beside(x):
    width = x.shape[-1]
    lane = lax.broadcasted_iota(jnp.int32, x.shape, x.ndim - 1)
    left = jnp.where(lane == 0, 0.0, pltpu.roll(x, 1, x.ndim - 1))
    right = jnp.where(lane == width - 1, 0.0, pltpu.roll(x, width - 1, x.ndim - 1))
    return left + right


def ranked(source_device, capacity):
    blocks = source_device.shape[0]
    devices = [source_device[block] for block in range(blocks)]
    found = []
    for block in range(blocks):
        rank = jnp.int32(0)
        for earlier in range(block):
            rank = rank + (devices[earlier] == devices[block]).astype(jnp.int32)
        found.append(devices[block] * capacity + rank)
    return found


def apply_kernel(
    spaces,
    slots,
    capacity,
    members,
    control_hbm,
    hybrid_weight,
    member_weights,
    source_device,
    source_row,
    arrived,
    perm,
    states,
    control,
    weight,
    blend,
    request,
    edges,
    stage_up,
    stage_down,
    recv_low,
    recv_high,
    ctrl_low,
    ctrl_high,
    ext_x,
    buf_a,
    buf_b,
    stat_a,
    stat_b,
    acc,
    red,
    ext,
    from_low,
    from_high,
    fin,
    asked,
    outgoing,
    load_sem,
    ctrl_sem,
    up_send,
    up_recv,
    down_send,
    down_recv,
    edge_send,
    edge_recv,
    ask_send,
    ask_recv,
    red_send,
    red_recv,
    fix_send,
    fix_recv,
    out_send,
    out_recv,
    own_sem,
):
    me = lax.axis_index("space")
    slot = lax.axis_index("member")
    count, chans, rows, width = members.shape
    own_chans = chans // slots
    parts, some = acc.shape[0], acc.shape[3]
    chunks = parts * slots
    has_low = me > 0
    has_high = me < spaces - 1
    low_mask = jnp.where(has_low, 1.0, 0.0).astype(jnp.float32)
    high_mask = jnp.where(has_high, 1.0, 0.0).astype(jnp.float32)
    low, high = {"space": me - 1}, {"space": me + 1}

    def first_chan(chunk):
        owner = lax.rem(slot + 1 + chunk % slots, slots)
        return owner * own_chans + (chunk // slots) * some

    def load(chunk):
        return pltpu.make_async_copy(
            members.at[:, pl.ds(first_chan(chunk), some)], states.at[chunk], load_sem.at[chunk]
        )

    def load_control():
        return pltpu.make_async_copy(control_hbm, control, ctrl_sem)

    load_control().start()
    for chunk in range(chunks):
        load(chunk).start()

    barrier = pltpu.get_barrier_semaphore()
    for step in range(1, spaces):
        pl.semaphore_signal(
            barrier, inc=1, device_id={"space": lax.rem(me + step, spaces)}, device_id_type=MESH
        )
    for step in range(1, slots):
        pl.semaphore_signal(
            barrier, inc=1, device_id={"member": lax.rem(slot + step, slots)}, device_id_type=MESH
        )

    place = lax.broadcasted_iota(jnp.int32, perm.shape, 0)
    source = lax.broadcasted_iota(jnp.int32, perm.shape, 1)
    wanted = lax.rem(place, count) * rows + place // count
    perm[...] = jnp.where(source == wanted, 1.0, 0.0).astype(jnp.bfloat16)

    load_control().wait()
    edges[0] = control[:, :REACH, :]
    edges[1] = control[:, rows - REACH :, :]
    pl.semaphore_wait(barrier, spaces + slots - 2)

    def remote(src, dst, send, recv, device):
        return pltpu.make_async_remote_copy(
            src_ref=src,
            dst_ref=dst,
            send_sem=send,
            recv_sem=recv,
            device_id=device,
            device_id_type=MESH,
        )

    def edge_up():
        return remote(edges.at[0], ctrl_high, edge_send.at[0], edge_recv.at[0], low)

    def edge_down():
        return remote(edges.at[1], ctrl_low, edge_send.at[1], edge_recv.at[1], high)

    def halo_up(turn):
        return remote(
            stage_up.at[turn], recv_high.at[turn], up_send.at[turn], up_recv.at[turn], low
        )

    def halo_down(turn):
        return remote(
            stage_down.at[turn], recv_low.at[turn], down_send.at[turn], down_recv.at[turn], high
        )

    def ask(step):
        target = lax.rem(me + step, spaces)
        return remote(
            request.at[target],
            asked.at[step - 1],
            ask_send.at[step - 1],
            ask_recv.at[step - 1],
            {"space": target},
        )

    @pl.when(has_low)
    def _():
        edge_up().start()

    @pl.when(has_high)
    def _():
        edge_down().start()

    span = REACH * count

    def send_edges(chunk, index):
        turn = chunk * some + index
        flat = states[chunk, :, index].reshape(count * rows, width)
        picks = jnp.concatenate(
            [perm[pl.ds(0, span), :], perm[pl.ds((rows - REACH) * count, span), :]], axis=0
        )
        both = jnp.dot(picks, flat, preferred_element_type=jnp.float32)
        stage_up[turn] = both[:span]
        stage_down[turn] = both[span:]

        @pl.when(has_low)
        def _():
            halo_up(turn).start()

        @pl.when(has_high)
        def _():
            halo_down(turn).start()

    for chunk in range(AHEAD):
        load(chunk).wait()

        def ahead(index, carry, chunk=chunk):
            send_edges(chunk, index)
            return carry

        lax.fori_loop(0, some, ahead, 0)

    shape = request.shape
    number = lax.broadcasted_iota(jnp.int32, shape, 0) * capacity
    number = number + lax.broadcasted_iota(jnp.int32, shape, 1)
    needs = jnp.zeros(shape, jnp.int32)
    for block, at in enumerate(ranked(source_device, capacity)):
        needs = jnp.where(number == at, source_row[block], needs)
    request[...] = needs
    for step in range(1, spaces):
        ask(step).start()

    total = lax.fori_loop(
        0,
        member_weights.shape[0],
        lambda index, so_far: so_far + member_weights[index],
        jnp.int32(0),
    )
    which = lax.broadcasted_iota(jnp.int32, weight.shape, 0)
    value = jnp.zeros(weight.shape, jnp.float32)
    for index in range(count):
        code = member_weights[slot * count + index].astype(jnp.float32)
        value = jnp.where(which == index, code, value)
    weight[...] = value / jnp.full(weight.shape, total.astype(jnp.float32)) * SCALE
    which = lax.broadcasted_iota(jnp.int32, blend.shape, 0)
    value = jnp.zeros(blend.shape, jnp.float32)
    for index in range(own_chans):
        value = jnp.where(which == index, hybrid_weight[slot * own_chans + index], value)
    blend[...] = value

    @pl.when(jnp.logical_not(has_low))
    def _():
        recv_low[...] = jnp.zeros_like(recv_low)
        ctrl_low[...] = jnp.zeros_like(ctrl_low)
        from_low[...] = jnp.zeros_like(from_low)

    @pl.when(jnp.logical_not(has_high))
    def _():
        recv_high[...] = jnp.zeros_like(recv_high)
        ctrl_high[...] = jnp.zeros_like(ctrl_high)
        from_high[...] = jnp.zeros_like(from_high)

    def swept(ref, at):
        middle = ref[at]
        return ref[at - 1] + ref[at + 1] + (middle + beside(middle))

    def masked(value, row):
        if row < 0:
            return value * low_mask
        if row >= rows:
            return value * high_mask
        return value

    stat_a[...] = jnp.zeros_like(stat_a)
    stat_b[...] = jnp.zeros_like(stat_b)
    margin = SWEEPS + 1
    for index in range(own_chans):
        field = control[slot * own_chans + index]
        for row in range(rows):
            stat_a[margin + row, pl.ds(index, 1), :] = field[row : row + 1]
    here, there = stat_a, stat_b
    for sweep in range(1, SWEEPS + 1):
        for row in range(-sweep, rows + sweep):
            there[margin + row] = masked(swept(here, margin + row), row)
        here, there = there, here
    static = here

    buf_a[...] = jnp.zeros_like(buf_a)
    buf_b[...] = jnp.zeros_like(buf_b)
    base = REACH + 2

    @pl.when(has_low)
    def _():
        edge_down().wait_recv()

    @pl.when(has_high)
    def _():
        edge_up().wait_recv()

    def give(part, group):
        return remote(
            acc.at[part, group],
            red.at[part, group],
            red_send.at[part, group],
            red_recv.at[part, group],
            {"member": lax.rem(slot + 1 + group, slots)},
        )

    def fix_up(part):
        return remote(
            ext.at[part, pl.ds(0, SWEEPS + 1)],
            from_high.at[part],
            fix_send.at[part, 0],
            fix_recv.at[part, 0],
            low,
        )

    def fix_down(part):
        return remote(
            ext.at[part, pl.ds(rows + SWEEPS, SWEEPS)],
            from_low.at[part],
            fix_send.at[part, 1],
            fix_recv.at[part, 1],
            high,
        )

    def answer(part, step):
        target = lax.rem(me + spaces - step, spaces)
        return remote(
            outgoing.at[part, step],
            arrived.at[part, me],
            out_send.at[part, step - 1],
            out_recv.at[part, step - 1],
            {"space": target},
        )

    def keep(part):
        return pltpu.make_async_copy(
            outgoing.at[part, 0], arrived.at[part, me], own_sem.at[part]
        )

    def combine(part):
        for group in range(slots - 1):
            give(part, group).wait_recv()
        mine = slice(part * some, (part + 1) * some)
        share = blend[mine, :]
        for row in range(-SWEEPS, rows + SWEEPS):
            value = (share * SCALE) * static[margin + row, mine, :]
            if -REACH <= row < rows + REACH:
                total = acc[part, slots - 1, row + REACH]
                for group in range(slots - 1):
                    total = total + red[part, group, row + REACH]
                value = value + (1.0 - share) * total
            ext[part, row + SWEEPS] = value

        @pl.when(has_low)
        def _():
            fix_up(part).start()

        @pl.when(has_high)
        def _():
            fix_down(part).start()

    def fill(part, step, wants):
        for place in range(capacity):
            line = jnp.concatenate([wants[place]] * (width // LANES), axis=1)
            line = jnp.broadcast_to(line, (some, width))
            lower, upper = fin[part, 0], fin[part, 1]
            for row in range(1, rows):
                hit = line == row
                lower = jnp.where(hit, fin[part, row], lower)
                upper = jnp.where(hit, fin[part, row + 1], upper)
            outgoing[part, step, place, 0] = lower
            outgoing[part, step, place, 1] = upper

    def serve(part):
        @pl.when(has_low)
        def _():
            fix_down(part).wait_recv()

        @pl.when(has_high)
        def _():
            fix_up(part).wait_recv()

        for row in range(rows + 1):
            value = ext[part, row + SWEEPS]
            if row < SWEEPS:
                value = value + from_low[part, row]
            if row >= rows - SWEEPS:
                value = value + from_high[part, row - rows + SWEEPS]
            fin[part, row] = value
        if part == 0:
            for step in range(1, spaces):
                ask(step).wait_recv()
        for step in sorted(range(1, spaces), key=lambda step: -min(step, spaces - step)):
            fill(part, step, [asked[step - 1, pl.ds(p, 1), :] for p in range(capacity)])
            answer(part, step).start()
        fill(part, 0, [request[me, pl.ds(p, 1), :] for p in range(capacity)])
        keep(part).start()

    for chunk in range(chunks):
        part, group = chunk // slots, chunk % slots
        if chunk + AHEAD < chunks:
            load(chunk + AHEAD).wait()

        def one_channel(index, carry, chunk=chunk, part=part, group=group):
            turn = chunk * some + index
            chan = first_chan(chunk) + index
            if chunk + AHEAD < chunks:
                send_edges(chunk + AHEAD, index)
            flat = states[chunk, :, index].reshape(count * rows, width)
            ext_x[pl.ds(span, rows * count), :] = jnp.dot(
                perm[...], flat, preferred_element_type=jnp.float32
            )

            @pl.when(has_low)
            def _():
                halo_down(turn).wait_recv()

            @pl.when(has_high)
            def _():
                halo_up(turn).wait_recv()

            ext_x[pl.ds(0, span), :] = recv_low[turn]
            ext_x[pl.ds((rows + REACH) * count, span), :] = recv_high[turn]

            def state(row):
                return ext_x[pl.ds((row + REACH) * count, count), :]

            for row in range(-REACH, rows + REACH):
                if row < 0:
                    line = ctrl_low[chan, pl.ds(row + REACH, 1), :]
                elif row >= rows:
                    line = ctrl_high[chan, pl.ds(row - rows, 1), :]
                else:
                    line = control[chan, pl.ds(row, 1), :]
                buf_a[base + row] = state(row) * line

            def collect(row, value):
                total = jnp.sum(state(row) * value * weight[...], axis=0, keepdims=True)
                acc[part, group, row + REACH, pl.ds(index, 1), :] = total

            for outer, inner, away in ((-1, 2, 1), (rows, rows - 3, -1)):
                near = buf_a[base + inner]
                far = buf_a[base + inner + away]
                collect(outer, SWEEPS * (near + beside(near)) + far)
                collect(outer - away, near)

            for row in range(-3, rows + 3):
                buf_b[base + row] = masked(swept(buf_a, base + row), row)
            for row in range(-2, rows + 2):
                buf_a[base + row] = masked(swept(buf_b, base + row), row)
            for row in range(-1, rows + 1):
                buf_b[base + row] = masked(swept(buf_a, base + row), row)
            for row in range(rows):
                collect(row, swept(buf_b, base + row))
            return carry

        lax.fori_loop(0, some, one_channel, 0)
        if group < slots - 1:
            give(part, group).start()
        else:
            combine(part)
        if group == 0 and part > 0:
            serve(part - 1)

    serve(parts - 1)

    for part in range(parts):
        for step in range(1, spaces):
            answer(part, step).wait_recv()
        keep(part).wait()
        for step in range(1, spaces):
            answer(part, step).wait_send()
        for group in range(slots - 1):
            give(part, group).wait_send()

        @pl.when(has_low)
        def _():
            fix_up(part).wait_send()

        @pl.when(has_high)
        def _():
            fix_down(part).wait_send()

    for step in range(1, spaces):
        ask(step).wait_send()

    @pl.when(has_low)
    def _():
        edge_up().wait_send()

    @pl.when(has_high)
    def _():
        edge_down().wait_send()

    def drain(turn, carry):
        @pl.when(has_low)
        def _():
            halo_up(turn).wait_send()

        @pl.when(has_high)
        def _():
            halo_down(turn).wait_send()

        return carry

    lax.fori_loop(0, chans, drain, 0)


def regrid_kernel(capacity, source_device, column_source, column_code, arrived, out, slot_index):
    blocks, fine = column_source.shape
    parts, some, width = arrived.shape[0], arrived.shape[3], arrived.shape[4]
    chans = parts * some
    tiles = width // LANES
    for block, at in enumerate(ranked(source_device, capacity)):
        slot_index[block] = at

    def one_group(group, carry):
        lines = pl.ds(pl.multiple_of(group * GROUP, GROUP), GROUP)
        sources = column_source[lines, :]
        codes = column_code[lines, :].astype(jnp.float32) / 16.0
        for inner in range(GROUP):
            block = group * GROUP + inner
            at = slot_index[block]
            lower = jnp.concatenate([arrived[part, at, 0] for part in range(parts)], axis=0)
            upper = jnp.concatenate([arrived[part, at, 1] for part in range(parts)], axis=0)
            pair = (0.75 * lower + 0.25 * upper, 0.25 * lower + 0.75 * upper)
            for tile in range(fine // LANES):
                columns = slice(tile * LANES, (tile + 1) * LANES)
                spread = (chans, LANES)
                left = jnp.broadcast_to(sources[inner : inner + 1, columns], spread)
                right_weight = jnp.broadcast_to(codes[inner : inner + 1, columns], spread)
                first = max(0, (tile * LANES - 1) // 2 - 2) // LANES
                last = min(width - 1, ((tile + 1) * LANES - 2) // 2 + 3) // LANES

                def value(field, index):
                    found = None
                    for piece in range(first, min(last, tiles - 1) + 1):
                        got = jnp.take_along_axis(
                            field[:, piece * LANES : (piece + 1) * LANES],
                            index & (LANES - 1),
                            axis=1,
                        )
                        if found is None:
                            found = got
                        else:
                            found = jnp.where(index >= piece * LANES, got, found)
                    return found

                for half in range(2):
                    out[block, :, half, columns] = (1.0 - right_weight) * value(
                        pair[half], left
                    ) + right_weight * value(pair[half], left + 1)
        return carry

    lax.fori_loop(0, blocks // GROUP, one_group, 0)


def per_device(
    members,
    control,
    hybrid_weight,
    member_weights,
    source_device,
    source_row,
    column_source,
    column_code,
):
    count, chans, rows, width = members.shape
    spaces, slots = lax.axis_size("space"), lax.axis_size("member")
    own_chans = chans // slots
    some = own_chans // PARTS
    chunks = PARTS * slots
    capacity = max(2, 2 * rows // spaces)
    f32 = jnp.float32
    source = source_device[:, 0]

    vmem = pl.BlockSpec(memory_space=pltpu.VMEM)
    smem = pl.BlockSpec(memory_space=pltpu.SMEM)
    anywhere = pl.BlockSpec(memory_space=pl.ANY)
    dma = pltpu.SemaphoreType.DMA
    halo = pltpu.VMEM((chans, REACH * count, width), f32)
    line = pltpu.VMEM((chans, REACH, width), f32)
    ext_rows = rows + 2 * REACH
    field = pltpu.VMEM((rows + 2 * (REACH + 2), count, width), f32)
    still = pltpu.VMEM((rows + 2 * (SWEEPS + 1), own_chans, width), f32)
    arrived = pl.pallas_call(
        functools.partial(apply_kernel, spaces, slots, capacity),
        out_shape=jax.ShapeDtypeStruct((PARTS, spaces, capacity, 2, some, width), f32),
        in_specs=[anywhere] * 2 + [smem] * 4,
        out_specs=anywhere,
        scratch_shapes=[
            pltpu.VMEM((rows * count, rows * count), jnp.bfloat16),
            pltpu.VMEM((chunks, count, some, rows, width), jnp.bfloat16),
            pltpu.VMEM((chans, rows, width), f32),
            pltpu.VMEM((count, width), f32),
            pltpu.VMEM((own_chans, width), f32),
            pltpu.VMEM((spaces, capacity, LANES), jnp.int32),
            pltpu.VMEM((2, chans, REACH, width), f32),
            halo,
            halo,
            halo,
            halo,
            line,
            line,
            pltpu.VMEM((ext_rows * count, width), f32),
            field,
            field,
            still,
            still,
            pltpu.VMEM((PARTS, slots, ext_rows, some, width), f32),
            pltpu.VMEM((PARTS, slots - 1, ext_rows, some, width), f32),
            pltpu.VMEM((PARTS, rows + 2 * SWEEPS, some, width), f32),
            pltpu.VMEM((PARTS, SWEEPS, some, width), f32),
            pltpu.VMEM((PARTS, SWEEPS + 1, some, width), f32),
            pltpu.VMEM((PARTS, rows + 1, some, width), f32),
            pltpu.VMEM((spaces - 1, capacity, LANES), jnp.int32),
            pltpu.VMEM((PARTS, spaces, capacity, 2, some, width), f32),
            dma((chunks,)),
            dma,
            dma((chans,)),
            dma((chans,)),
            dma((chans,)),
            dma((chans,)),
            dma((2,)),
            dma((2,)),
            dma((spaces - 1,)),
            dma((spaces - 1,)),
            dma((PARTS, slots - 1)),
            dma((PARTS, slots - 1)),
            dma((PARTS, 2)),
            dma((PARTS, 2)),
            dma((PARTS, spaces - 1)),
            dma((PARTS, spaces - 1)),
            dma((PARTS,)),
        ],
        compiler_params=pltpu.CompilerParams(
            collective_id=0, has_side_effects=True, vmem_limit_bytes=48 * 2**20
        ),
        name="covariance_apply",
    )(members, control, hybrid_weight, member_weights, source, source_row)

    arrived = arrived.reshape(PARTS, spaces * capacity, 2, some, width)
    return pl.pallas_call(
        functools.partial(regrid_kernel, capacity),
        out_shape=jax.ShapeDtypeStruct((rows, own_chans, 2, column_source.shape[1]), f32),
        in_specs=[smem] + [vmem] * 3,
        out_specs=vmem,
        scratch_shapes=[pltpu.SMEM((rows,), jnp.int32)],
        compiler_params=pltpu.CompilerParams(vmem_limit_bytes=32 * 2**20),
        name="regrid",
    )(source, column_source, column_code, arrived)


def solution(mesh):
    placed = (
        P("member", None, "space", None),
        P(None, "space", None),
        P(),
        P(),
        P("space", None),
        P("space"),
        P("space", None),
        P("space", None),
    )
    return jax.shard_map(
        per_device,
        mesh=mesh,
        in_specs=placed,
        out_specs=P("space", "member", None, None),
        check_vma=False,
    )
```

time: 128 us -> 110 us (0.86)
  Pallas kernels: 117 us -> 106 us
  other arithmetic: 4.97 us -> 0 us
  local copies, waits for them, and re-layouts: 6.04 us -> 3.76 us
    pallas_call x2, Pallas kernels: 117 us -> 106 us  [the longest x1 102 us: per_device(): pl.pallas_call(functools.partial(apply_kernel, spaces, slots, capacity),...]
    reduce_sum x3 -> x0, other arithmetic: 2.91 us -> none  [the longest x1 1.26 us: per_device(): jnp.sum(codes)]
    unnamed x5 -> x14, local copies, waits for them, and re-layouts: 1.21 us -> 3.76 us
    broadcast_in_dim x6 -> x0, local copies, waits for them, and re-layouts: 1.97 us -> none  [the longest x1 0.84 us: per_device(): column_source[:, None]]
    dynamic_slice x2 -> x0, local copies, waits for them, and re-layouts: 1.67 us -> none  [the longest x1 0.95 us: per_device(): own = lax.dynamic_slice_in_dim(control, slot * own_chans, own_chans, 0)]
where the time goes in v1:
time: 110 us; the launch traced here: 109 us
  Pallas kernels  106 us (96%)
  local copies, waits for them, and re-layouts  3.76 us (3%)
    pallas_call x1, Pallas kernels, per_device(): pl.pallas_call(functools.partial(apply_kernel, spaces, slots, capacity),...  102 us
    unnamed x14, local copies, waits for them, and re-layouts  3.76 us
    pallas_call x1, Pallas kernels, per_device(): pl.pallas_call(functools.partial(regrid_kernel, capacity), out_shape=jax....  3.27 us

profile of v1, /device:TPU:0, one launch (start us, length us, event | category | flops | bytes accessed | tf_op | source)
XLA Modules:
  0.0 109.5 jit_solution(9284823686887617050)
XLA Ops:
  0.0 0.0 copy-start
  0.0 1.1 %copy-done = f32[32,16,384]{2,1,0:T(8,128)S(1)} copy-done((f32[32,16,384]{2,1,0:T(8,128)S(1)}, f32[32,16,384]{2,1,0:T(8,128)}, u32[]{:S(2)}) %copy-start) | copy-done | bytes 786456
  1.1 0.0 copy-start.3
  1.1 0.7 copy-done.3
  1.8 0.0 copy-start.4
  1.8 0.7 copy-done.4
  2.4 0.0 copy-start.5
  2.4 0.7 copy-done.5
  3.1 0.0 copy-start.6
  3.1 0.7 copy-done.6
  3.8 0.0 copy-start.1
  3.8 0.0 copy-start.2
  3.8 102.4 %covariance_apply.1 = f32[2,8,4,2,4,384]{5,4,3,2,1,0:T(4,128)S(1)} custom-call(bf16[16,32,16,384]{3,2,1,0:T(8,128)(2,1)} %members.1, f32[32,16,384]{2,1,0:T(8,128)S(1)} %copy-done, f32[32]{0:T(128)S(1)} %copy-done.4, s32[64]{0:T(128)S(1)} %copy-done.5, s32[16]{0:T(128)S(1)} %bitcast.3, s32[16]{0:T(128)S(1)} %copy-done.6), custom_call_target="tpu_custom_call" | custom-call | tf_op jit(solution)/shard_map/covariance_apply/pallas_call | solution.py:582
  106.2 0.0 copy-done.1
  106.2 0.0 copy-done.2
  106.2 3.3 %regrid.1 = f32[16,8,2,768]{3,2,1,0:T(2,128)} custom-call(s32[16]{0:T(128)S(1)} %bitcast.4, s32[16,768]{1,0:T(8,128)S(1)} %copy-done.1, s32[16,768]{1,0:T(8,128)S(1)} %copy-done.2, f32[2,32,2,4,384]{4,3,2,1,0:T(4,128)S(1)} %bitcast.2), custom_call_target="tpu_custom_call" | custom-call | tf_op jit(solution)/shard_map/regrid/pallas_call | solution.py:639
Async XLA Ops:
  0.0 1.1 %copy-start = (f32[32,16,384]{2,1,0:T(8,128)S(1)}, f32[32,16,384]{2,1,0:T(8,128)}, u32[]{:S(2)}) copy-start(f32[32,16,384]{2,1,0:T(8,128)} %control_hbm.1) | copy-start | bytes 2359300
  1.1 0.7 copy-start.3
  1.8 0.7 copy-start.4
  2.4 0.7 copy-start.5
  3.1 0.7 copy-start.6
  3.8 102.4 %copy-start.1 = (s32[16,768]{1,0:T(8,128)S(1)}, s32[16,768]{1,0:T(8,128)}, u32[]{:S(2)}) copy-start(s32[16,768]{1,0:T(8,128)} %column_source.1) | copy-start | bytes 147460
  3.8 102.5 %copy-start.2 = (s32[16,768]{1,0:T(8,128)S(1)}, s32[16,768]{1,0:T(8,128)}, u32[]{:S(2)}) copy-start(s32[16,768]{1,0:T(8,128)} %column_code.1) | copy-start | bytes 147460

commit v2 on v1

--- a/solution.py
+++ b/solution.py
@@ -14,16 +14,22 @@
 LANES = 128
 GROUP = 8
 PARTS = 2
-AHEAD = 1
+AHEAD = 2
 MESH = pl.DeviceIdType.MESH
 
 
 def beside(x):
-    width = x.shape[-1]
-    lane = lax.broadcasted_iota(jnp.int32, x.shape, x.ndim - 1)
-    left = jnp.where(lane == 0, 0.0, pltpu.roll(x, 1, x.ndim - 1))
-    right = jnp.where(lane == width - 1, 0.0, pltpu.roll(x, width - 1, x.ndim - 1))
-    return left + right
+    tiles = x.shape[1] // LANES
+    lane = lax.broadcasted_iota(jnp.int32, (x.shape[0], LANES), 1)
+    pieces = [x[:, tile * LANES : (tile + 1) * LANES] for tile in range(tiles)]
+    ahead = [pltpu.roll(piece, 1, 1) for piece in pieces]
+    behind = [pltpu.roll(piece, LANES - 1, 1) for piece in pieces]
+    found = []
+    for tile in range(tiles):
+        left = jnp.where(lane == 0, ahead[tile - 1] if tile else 0.0, ahead[tile])
+        after = behind[tile + 1] if tile + 1 < tiles else 0.0
+        found.append(left + jnp.where(lane == LANES - 1, after, behind[tile]))
+    return jnp.concatenate(found, axis=1)
 
 
 def ranked(source_device, capacity):
@@ -44,25 +50,27 @@
     capacity,
     members,
     control_hbm,
+    hybrid_hbm,
+    weights_hbm,
+    device_hbm,
+    row_hbm,
+    arrived,
+    perm,
+    states,
+    control,
     hybrid_weight,
     member_weights,
     source_device,
     source_row,
-    arrived,
-    perm,
-    states,
-    control,
     weight,
     blend,
     request,
     edges,
-    stage_up,
-    stage_down,
+    turned,
     recv_low,
     recv_high,
     ctrl_low,
     ctrl_high,
-    ext_x,
     buf_a,
     buf_b,
     stat_a,
@@ -77,6 +85,7 @@
     outgoing,
     load_sem,
     ctrl_sem,
+    small_sem,
     up_send,
     up_recv,
     down_send,
@@ -117,7 +126,21 @@
     def load_control():
         return pltpu.make_async_copy(control_hbm, control, ctrl_sem)
 
+    def load_small():
+        pairs = (
+            (hybrid_hbm, hybrid_weight),
+            (weights_hbm, member_weights),
+            (device_hbm, source_device),
+            (row_hbm, source_row),
+        )
+        return [
+            pltpu.make_async_copy(src, dst, small_sem.at[index])
+            for index, (src, dst) in enumerate(pairs)
+        ]
+
     load_control().start()
+    for copy in load_small():
+        copy.start()
     for chunk in range(chunks):
         load(chunk).start()
 
@@ -157,14 +180,20 @@
     def edge_down():
         return remote(edges.at[1], ctrl_low, edge_send.at[1], edge_recv.at[1], high)
 
+    span = REACH * count
+
     def halo_up(turn):
         return remote(
-            stage_up.at[turn], recv_high.at[turn], up_send.at[turn], up_recv.at[turn], low
+            turned.at[turn, pl.ds(0, span)], recv_high.at[turn], up_send.at[turn], up_recv.at[turn], low
         )
 
     def halo_down(turn):
         return remote(
-            stage_down.at[turn], recv_low.at[turn], down_send.at[turn], down_recv.at[turn], high
+            turned.at[turn, pl.ds((rows - REACH) * count, span)],
+            recv_low.at[turn],
+            down_send.at[turn],
+            down_recv.at[turn],
+            high,
         )
 
     def ask(step):
@@ -185,17 +214,14 @@
     def _():
         edge_down().start()
 
-    span = REACH * count
+    def turn_over(chunk, index):
+        flat = states[chunk, :, index].reshape(count * rows, width)
+        turned[chunk * some + index] = jnp.dot(
+            perm[...], flat, preferred_element_type=jnp.float32
+        )
 
     def send_edges(chunk, index):
         turn = chunk * some + index
-        flat = states[chunk, :, index].reshape(count * rows, width)
-        picks = jnp.concatenate(
-            [perm[pl.ds(0, span), :], perm[pl.ds((rows - REACH) * count, span), :]], axis=0
-        )
-        both = jnp.dot(picks, flat, preferred_element_type=jnp.float32)
-        stage_up[turn] = both[:span]
-        stage_down[turn] = both[span:]
 
         @pl.when(has_low)
         def _():
@@ -209,10 +235,13 @@
         load(chunk).wait()
 
         def ahead(index, carry, chunk=chunk):
+            turn_over(chunk, index)
             send_edges(chunk, index)
             return carry
 
         lax.fori_loop(0, some, ahead, 0)
+    for copy in load_small():
+        copy.wait()
 
     shape = request.shape
     number = lax.broadcasted_iota(jnp.int32, shape, 0) * capacity
@@ -400,12 +429,6 @@
         def one_channel(index, carry, chunk=chunk, part=part, group=group):
             turn = chunk * some + index
             chan = first_chan(chunk) + index
-            if chunk + AHEAD < chunks:
-                send_edges(chunk + AHEAD, index)
-            flat = states[chunk, :, index].reshape(count * rows, width)
-            ext_x[pl.ds(span, rows * count), :] = jnp.dot(
-                perm[...], flat, preferred_element_type=jnp.float32
-            )
 
             @pl.when(has_low)
             def _():
@@ -415,11 +438,12 @@
             def _():
                 halo_up(turn).wait_recv()
 
-            ext_x[pl.ds(0, span), :] = recv_low[turn]
-            ext_x[pl.ds((rows + REACH) * count, span), :] = recv_high[turn]
-
             def state(row):
-                return ext_x[pl.ds((row + REACH) * count, count), :]
+                if row < 0:
+                    return recv_low[turn, pl.ds((row + REACH) * count, count), :]
+                if row >= rows:
+                    return recv_high[turn, pl.ds((row - rows) * count, count), :]
+                return turned[turn, pl.ds(row * count, count), :]
 
             for row in range(-REACH, rows + REACH):
                 if row < 0:
@@ -448,6 +472,9 @@
                 buf_b[base + row] = masked(swept(buf_a, base + row), row)
             for row in range(rows):
                 collect(row, swept(buf_b, base + row))
+            if chunk + AHEAD < chunks:
+                turn_over(chunk + AHEAD, index)
+                send_edges(chunk + AHEAD, index)
             return carry
 
         lax.fori_loop(0, some, one_channel, 0)
@@ -582,23 +609,25 @@
     arrived = pl.pallas_call(
         functools.partial(apply_kernel, spaces, slots, capacity),
         out_shape=jax.ShapeDtypeStruct((PARTS, spaces, capacity, 2, some, width), f32),
-        in_specs=[anywhere] * 2 + [smem] * 4,
+        in_specs=[pl.BlockSpec(memory_space=pltpu.HBM)] * 6,
         out_specs=anywhere,
         scratch_shapes=[
             pltpu.VMEM((rows * count, rows * count), jnp.bfloat16),
             pltpu.VMEM((chunks, count, some, rows, width), jnp.bfloat16),
             pltpu.VMEM((chans, rows, width), f32),
+            pltpu.SMEM(hybrid_weight.shape, f32),
+            pltpu.SMEM(member_weights.shape, jnp.int32),
+            pltpu.SMEM(source.shape, jnp.int32),
+            pltpu.SMEM(source.shape, jnp.int32),
             pltpu.VMEM((count, width), f32),
             pltpu.VMEM((own_chans, width), f32),
             pltpu.VMEM((spaces, capacity, LANES), jnp.int32),
             pltpu.VMEM((2, chans, REACH, width), f32),
-            halo,
-            halo,
+            pltpu.VMEM((chans, rows * count, width), f32),
             halo,
             halo,
             line,
             line,
-            pltpu.VMEM((ext_rows * count, width), f32),
             field,
             field,
             still,
@@ -613,6 +642,7 @@
             pltpu.VMEM((PARTS, spaces, capacity, 2, some, width), f32),
             dma((chunks,)),
             dma,
+            dma((4,)),
             dma((chans,)),
             dma((chans,)),
             dma((chans,)),
@@ -630,7 +660,7 @@
             dma((PARTS,)),
         ],
         compiler_params=pltpu.CompilerParams(
-            collective_id=0, has_side_effects=True, vmem_limit_bytes=48 * 2**20
+            collective_id=0, has_side_effects=True, vmem_limit_bytes=64 * 2**20
         ),
         name="covariance_apply",
     )(members, control, hybrid_weight, member_weights, source, source_row)

time: 110 us -> 109 us (level)
    unnamed x14 -> x8, local copies, waits for them, and re-layouts: 3.76 us -> 3.38 us
where the time goes in v2:
time: 109 us
  Pallas kernels  105 us (96%)
  local copies, waits for them, and re-layouts  3.38 us (3%)
    pallas_call x1, Pallas kernels, per_device(): pl.pallas_call(functools.partial(apply_kernel, spaces, slots, capacity),...  102 us
    unnamed x8, local copies, waits for them, and re-layouts  3.38 us
    pallas_call x1, Pallas kernels, per_device(): pl.pallas_call(functools.partial(regrid_kernel, capacity), out_shape=jax....  3.26 us

profile of v2, /device:TPU:0, one launch (start us, length us, event | category | flops | bytes accessed | tf_op | source)
XLA Modules:
  0.0 108.7 jit_solution(10380387996203352123)
XLA Ops:
  0.0 102.0 %covariance_apply.1 = f32[2,8,4,2,4,384]{5,4,3,2,1,0:T(4,128)} custom-call(bf16[16,32,16,384]{3,2,1,0:T(8,128)(2,1)} %members.1, f32[32,16,384]{2,1,0:T(8,128)} %control_hbm.1, f32[32]{0:T(128)} %hybrid_hbm.1, s32[64]{0:T(128)} %weights_hbm.1, s32[16]{0:T(128)} %bitcast.3, s32[16]{0:T(128)} %row_hbm.1), custom_call_target="tpu_custom_call" | custom-call | tf_op jit(solution)/shard_map/covariance_apply/pallas_call | solution.py:609
  102.0 0.0 copy-start
  102.0 1.1 %copy-done = f32[2,8,4,2,4,384]{5,4,3,2,1,0:T(4,128)S(1)} copy-done((f32[2,8,4,2,4,384]{5,4,3,2,1,0:T(4,128)S(1)}, f32[2,8,4,2,4,384]{5,4,3,2,1,0:T(4,128)}, u32[]{:S(2)}) %copy-start) | copy-done | bytes 786456
  103.1 0.0 copy-start.1
  103.1 0.8 copy-done.1
  103.9 0.0 copy-start.2
  103.9 0.8 copy-done.2
  104.7 0.0 copy-start.3
  104.7 0.7 copy-done.3
  105.4 3.3 %regrid.1 = f32[16,8,2,768]{3,2,1,0:T(2,128)} custom-call(s32[16]{0:T(128)S(1)} %bitcast.4, s32[16,768]{1,0:T(8,128)S(1)} %copy-done.1, s32[16,768]{1,0:T(8,128)S(1)} %copy-done.2, f32[2,32,2,4,384]{4,3,2,1,0:T(4,128)S(1)} %bitcast.2), custom_call_target="tpu_custom_call" | custom-call | tf_op jit(solution)/shard_map/regrid/pallas_call | solution.py:669
Async XLA Ops:
  102.0 1.1 %copy-start = (f32[2,8,4,2,4,384]{5,4,3,2,1,0:T(4,128)S(1)}, f32[2,8,4,2,4,384]{5,4,3,2,1,0:T(4,128)}, u32[]{:S(2)}) copy-start(f32[2,8,4,2,4,384]{5,4,3,2,1,0:T(4,128)} %covariance_apply.1) | copy-start | bytes 2359300
  103.1 0.8 copy-start.1
  103.9 0.8 copy-start.2
  104.7 0.7 copy-start.3
